TPU v7x, 512 devices: a whole 4x8x8 slice. The times are simulated.
512 devices in a mesh: row: 64 (over y, x, core), col: 8 (over z).
Axes of the slice: x: 4, y: 8, z: 8, core: 2. Of those that a mesh axis runs over, the one named last changes fastest.
Arguments:
- hidden_states: bfloat16 [16384, 8192], P('row', 'col'), may hold values from -80 to 80, as said below
- sketch_matrix: bfloat16 [8192, 512], P('col'), may hold values from -0.0625 to 0.0625
Outputs:
- q_left: float32 [16384, 512], P(('row', 'col'))
- q_right: float32 [8, 1024, 512], P('col', 'row')
- triangle: float32 [512, 512], replicated
Inputs may be any that keep to these rules, and one draw needn't show every extreme that they name: `hidden_states`: real-valued activation rows.
All inputs are finite; a program needn't handle non-finite values.
Results may differ from a plain program's by a relative error of at most 0.0023.
Values may be sent and summed in bfloat16 or wider, within the bound.
No kernel may reach another device: no remote copies, remote signals or barrier semaphores. Data moves between devices by JAX's collectives and lax.ppermute only.
A program may use at most 64 MiB of HBM per device.

v0:
```python
import math

import jax
import jax.numpy as jnp
from jax import lax
from jax.sharding import PartitionSpec as P


def factorize(gram):
    return jnp.linalg.cholesky(gram)


def substitute(lower, tall):
    return jax.scipy.linalg.solve_triangular(lower, tall.T, lower=True).T


def gram_of(tall):
    return jnp.dot(
        tall.T, tall, precision=lax.Precision.HIGHEST, preferred_element_type=jnp.float32
    )


def per_device(hidden_states, sketch_matrix):
    local_rows, block_width = hidden_states.shape
    col_groups = lax.axis_size("col")
    row_groups = lax.axis_size("row")
    share_rows = local_rows // col_groups
    total_rows = local_rows * row_groups
    total_width = block_width * col_groups
    partial_sketch = jnp.dot(hidden_states, sketch_matrix, preferred_element_type=jnp.float32)
    sketch_whole = lax.psum(partial_sketch, "col")
    own_sketch = lax.dynamic_slice_in_dim(
        sketch_whole, lax.axis_index("col") * share_rows, share_rows, 0
    )
    gram_left = lax.psum(gram_of(own_sketch), ("row", "col"))
    low_left = factorize(gram_left)
    basis_every = substitute(low_left, sketch_whole)
    basis_own = lax.dynamic_slice_in_dim(
        basis_every, lax.axis_index("col") * share_rows, share_rows, 0
    )
    basis_half = basis_every.astype(jnp.bfloat16)
    image_share = block_width // row_groups
    image = lax.psum_scatter(
        lax.dot_general(
            hidden_states, basis_half, (((0,), (0,)), ((), ())), preferred_element_type=jnp.float32
        ),
        "row",
        scatter_dimension=0,
        tiled=True,
    )
    gram_right = lax.psum(gram_of(image), ("row", "col"))
    low_right = factorize(gram_right)
    right_basis = substitute(low_right, image)
    q_left = basis_own * math.sqrt(total_rows)
    q_right = (right_basis * math.sqrt(total_width)).reshape(1, image_share, right_basis.shape[1])
    triangle = low_right / math.sqrt(total_width)
    return (q_left, q_right, triangle)


def solution(mesh):
    placed = (P("row", "col"), P("col", None))
    return jax.shard_map(
        per_device,
        mesh=mesh,
        in_specs=placed,
        out_specs=(P(("row", "col"), None), P("col", "row", None), P()),
        check_vma=False,
    )
```

profile of v0, /device:TPU:1, one launch (start us, length us, event | category | flops | bytes accessed | tf_op | source)
XLA Modules:
  0.0 1103.7 jit_solution(14392766160905359920)
XLA Ops:
  7.2 1.2 copy-done
  8.4 2.3 fusion.69
  10.7 81.0 %all-reduce.5.cloned.1.call-done = f32[256,512]{1,0:T(8,128)} async-done(((f32[256,512]{1,0:T(8,128)}), f32[256,512]{1,0:T(8,128)}) %all-reduce.5.cloned.1.call-update) | async-done | bytes 524304 | tf_op jit(solution)/shard_map/psum | solution.py:31
  91.7 2.9 fusion.51
  94.7 278.6 %all-reduce.7.cloned.1.call-done = f32[512,512]{0,1:T(8,128)} async-done(((f32[512,512]{0,1:T(8,128)}), f32[512,512]{0,1:T(8,128)}) %all-reduce.7.cloned.1.call-update) | async-done | bytes 1048592 | tf_op jit(solution)/shard_map/psum | solution.py:35
  373.3 1.6 copy.11
  375.2 1.0 copy-done.3
  376.2 11.7 %cholesky.286 = f32[128,128]{1,0:T(8,128)S(1)} custom-call(f32[128,128]{1,0:T(8,128)S(1)} %cholesky.426), custom_call_target="Cholesky" | custom-call | tf_op jit(solution)/shard_map/jit(cholesky)/cholesky | solution.py:10
  388.1 9.8 custom-call.33
  397.9 1.2 constant_dynamic-update-slice_fusion.3
  399.1 1.3 convolution_subtract_fusion.1
  400.4 11.7 %cholesky.305 = f32[128,128]{1,0:T(8,128)S(1)} custom-call(f32[128,128]{1,0:T(8,128)S(1)} %cholesky.430), custom_call_target="Cholesky" | custom-call | tf_op jit(solution)/shard_map/jit(cholesky)/cholesky | solution.py:10
  412.2 10.0 custom-call.34
  422.5 1.3 convolution_subtract_fusion.5
  423.8 11.7 %cholesky.326 = f32[128,128]{1,0:T(8,128)S(1)} custom-call(f32[128,128]{1,0:T(8,128)S(1)} %cholesky.435), custom_call_target="Cholesky" | custom-call | tf_op jit(solution)/shard_map/jit(cholesky)/cholesky | solution.py:10
  435.5 9.8 custom-call.35
  445.6 1.2 convolution_subtract_fusion.11
  446.8 11.7 %cholesky.343 = f32[128,128]{1,0:T(8,128)S(1)} custom-call(f32[128,128]{1,0:T(8,128)S(1)} %convolution_subtract_fusion.11), custom_call_target="Cholesky" | custom-call | tf_op jit(solution)/shard_map/jit(cholesky)/cholesky | solution.py:10
  458.5 0.7 compare_reduce_fusion.5
  459.3 0.6 compare_reduce_fusion.4
  459.9 0.7 compare_reduce_fusion.6
  463.1 12.4 %select_select_fusion = f32[512,512]{1,0:T(8,128)S(1)} fusion(f32[512,512]{1,0:T(8,128)S(1)} %get-tuple-element.59, pred[]{:T(512)S(6)} %cholesky.348), kind=kLoop, calls=%fused_computation.5 | loop fusion | flops 1048576 | bytes 2097153 | tf_op jit(solution)/shard_map/jit(_solve_triangular)/triangular_solve | solution.py:14
  475.6 8.5 while.2
  476.3 1.4 bitcast_dynamic-update-slice_fusion.4
  478.4 1.4 bitcast_dynamic-update-slice_fusion.4
  480.5 1.4 bitcast_dynamic-update-slice_fusion.4
  482.6 1.4 bitcast_dynamic-update-slice_fusion.4
  484.1 39.3 %custom-call.28 = f32[4,128,128]{1,2,0:T(8,128)S(1)} custom-call(f32[4,128,128]{2,1,0:T(8,128)S(1)} %get-tuple-element.11), custom_call_target="InvertDiagBlocksLowerTriangular" | custom-call | tf_op jit(solution)/shard_map/jit(_solve_triangular)/triangular_solve | solution.py:14
  523.4 1.2 fusion.27
  524.6 1.3 convolution_subtract_fusion.6
  527.2 0.8 convolution_subtract_fusion.3
  528.3 0.6 copy-done.5
  529.0 1.5 convolution_bitcast_fusion
  530.4 1.9 copy.17
  532.4 140.0 %reduce-scatter.4.cloned.1.call-done = f32[16,512]{1,0:T(8,128)} async-done(((f32[1024,512]{1,0:T(8,128)}), f32[16,512]{1,0:T(8,128)}) %reduce-scatter.4.cloned.1.call-update) | async-done | bytes 32784
  672.4 2.9 fusion.70
  675.5 0.7 copy.14
  676.3 278.6 %all-reduce.9.cloned.1.call-done = f32[512,512]{0,1:T(8,128)} async-done(((f32[512,512]{0,1:T(8,128)}), f32[512,512]{0,1:T(8,128)}) %all-reduce.9.cloned.1.call-update) | async-done | bytes 1048592 | tf_op jit(solution)/shard_map/psum | solution.py:51
  954.9 1.6 copy.13
  956.8 1.0 copy-done.4
  957.8 11.7 %cholesky.358 = f32[128,128]{1,0:T(8,128)S(1)} custom-call(f32[128,128]{1,0:T(8,128)S(1)} %cholesky.439), custom_call_target="Cholesky" | custom-call | tf_op jit(solution)/shard_map/jit(cholesky)/cholesky | solution.py:10
  969.7 9.8 custom-call.36
  979.5 1.2 constant_dynamic-update-slice_fusion.1
  980.7 1.3 convolution_subtract_fusion
  982.0 11.7 %cholesky.377 = f32[128,128]{1,0:T(8,128)S(1)} custom-call(f32[128,128]{1,0:T(8,128)S(1)} %cholesky.443), custom_call_target="Cholesky" | custom-call | tf_op jit(solution)/shard_map/jit(cholesky)/cholesky | solution.py:10
  993.8 10.0 custom-call.37
  1004.0 1.3 convolution_subtract_fusion.2
  1005.3 11.7 %cholesky.398 = f32[128,128]{1,0:T(8,128)S(1)} custom-call(f32[128,128]{1,0:T(8,128)S(1)} %cholesky.448), custom_call_target="Cholesky" | custom-call | tf_op jit(solution)/shard_map/jit(cholesky)/cholesky | solution.py:10
  1017.1 9.8 custom-call.38
  1027.1 1.2 convolution_subtract_fusion.10
  1028.3 11.9 %cholesky.415 = f32[128,128]{1,0:T(8,128)S(1)} custom-call(f32[128,128]{1,0:T(8,128)S(1)} %convolution_subtract_fusion.10), custom_call_target="Cholesky" | custom-call | tf_op jit(solution)/shard_map/jit(cholesky)/cholesky | solution.py:10
  1040.3 0.6 compare_reduce_fusion.3
  1041.0 0.7 compare_reduce_fusion.2
  1041.7 0.6 compare_reduce_fusion.1
  1042.3 0.7 compare_reduce_fusion
  1045.5 1.2 fusion.3
  1046.8 8.1 while.3
  1046.9 0.6 fusion.89
  1047.5 1.3 bitcast_dynamic-update-slice_fusion.5
  1049.5 1.3 bitcast_dynamic-update-slice_fusion.5
  1051.5 1.3 bitcast_dynamic-update-slice_fusion.5
  1053.6 1.3 bitcast_dynamic-update-slice_fusion.5
  1054.9 39.3 %custom-call.29 = f32[4,128,128]{1,2,0:T(8,128)S(1)} custom-call(f32[4,128,128]{2,1,0:T(8,128)S(1)} %get-tuple-element.19), custom_call_target="InvertDiagBlocksLowerTriangular" | custom-call | tf_op jit(solution)/shard_map/jit(_solve_triangular)/triangular_solve | solution.py:14
  1096.0 0.7 fusion.53
  (77 shorter events, 10.6 us)
Async XLA Ops:
  7.2 1.2 copy-start
  7.2 84.5 %all-reduce.5.cloned.1.call-start = ((), (), s32[]{:S(2)}) async-start(), calls=%async_computation.1 | async-start | bytes 1048576 | tf_op jit(solution)/shard_map/psum | solution.py:31
  10.7 362.6 %all-reduce.7.cloned.1.call-start = ((), (), s32[]{:S(2)}) async-start(), calls=%async_computation.2 | async-start | bytes 2097152 | tf_op jit(solution)/shard_map/psum | solution.py:35
  94.6 577.7 %reduce-scatter.4.cloned.1.call-start = ((), (), s32[]{:S(2)}) async-start(), calls=%async_computation.4 | async-start | bytes 2129920
  373.3 1.7 copy-start.2
  375.2 1.0 copy-start.3
  475.5 50.7 %copy-start.7 = (f32[256,512]{1,0:T(8,128)S(1)}, f32[256,512]{1,0:T(8,128)}, u32[]{:S(2)}) copy-start(f32[256,512]{1,0:T(8,128)} %all-reduce.5.cloned.1.call-done) | copy-start | bytes 1572868
  528.3 0.7 copy-start.5
  532.3 142.9 %copy-start.6 = (f32[128,256]{1,0:T(8,128)S(1)}, f32[128,256]{1,0:T(8,128)}, u32[]{:S(2)}) copy-start(f32[128,256]{1,0:T(8,128)} %copy-done.5) | copy-start | bytes 393220
  532.3 422.6 %all-reduce.9.cloned.1.call-start = ((), (), s32[]{:S(2)}) async-start(), calls=%async_computation.3 | async-start | bytes 2097152 | tf_op jit(solution)/shard_map/psum | solution.py:51
  672.4 3.8 copy-start.8
  954.9 1.7 copy-start.1
  956.8 1.0 copy-start.4
Sparse Core Ops, SparseCore 0:
  10.9 80.7 all-reduce.4
  98.1 275.1 all-reduce.6
  532.5 139.8 reduce-scatter.3
  678.7 276.2 all-reduce.8
where the time goes:
time: 1110 us; the launch traced here: 1100 us
  waiting for transfers between devices  778 us (70%)
  other arithmetic  252 us (23%)
  matrix products  27 us (2%)
  local copies, waits for them, and re-layouts  26.6 us (2%)
  between operations  19.7 us (2%)
    psum x1, waiting for transfers between devices, per_device(): gram_left = lax.psum(gram_of(own_sketch), ('row', 'col'))  279 us
    psum x1, waiting for transfers between devices, per_device(): gram_right = lax.psum(gram_of(image), ('row', 'col'))  279 us
    another operation x29, other arithmetic, factorize(): return jnp.linalg.cholesky(gram)  158 us
    unnamed x5, waiting for transfers between devices  140 us
    another operation x5, other arithmetic, substitute(): return jax.scipy.linalg.solve_triangular(lower, tall.T, lower=True).T  91.1 us
    psum x1, waiting for transfers between devices, per_device(): sketch_whole = lax.psum(partial_sketch, 'col')  81 us
  transfers between devices with their start and end apart: 4, of which 4 were waited for; matrix products, arithmetic and copies ran while one was open for 0% of the time, Pallas kernels for 0%

commit v1 on v0

v1 whole, which is shorter than its diff:
```python
import functools
import math

import jax
import jax.numpy as jnp
from jax import lax
from jax.experimental import pallas as pl
from jax.experimental.pallas import tpu as pltpu
from jax.sharding import Mesh
from jax.sharding import PartitionSpec as P

HIGHEST = lax.Precision.HIGHEST
BLOCK = 128
RANK = 8
ROW = ("y", "x", "core")


def across_lanes(piece, column):
    return jnp.broadcast_to(piece[:, column : column + 1], piece.shape)


def across_rows(piece, row):
    return jnp.broadcast_to(piece[row : row + 1, :], piece.shape)


def inverse_factor(block):
    groups = BLOCK // 8
    row = lax.broadcasted_iota(jnp.int32, (8, BLOCK), 0)
    lane = lax.broadcasted_iota(jnp.int32, (8, BLOCK), 1)
    left = [block[8 * i : 8 * i + 8, :] for i in range(groups)]
    right = [jnp.where(lane == row + 8 * i, 1.0, 0.0) for i in range(groups)]
    finished = [jnp.zeros((8, BLOCK), jnp.float32) for _ in range(groups)]
    for first in range(0, BLOCK, RANK):
        group, offset = divmod(first, 8)
        columns = [across_lanes(left[group], first + t) for t in range(RANK)]
        pivot = [[across_rows(columns[u], offset + t) for u in range(t + 1)] for t in range(RANK)]
        on_left = [across_rows(left[group], offset + t) for t in range(RANK)]
        on_right = [across_rows(right[group], offset + t) for t in range(RANK)]
        lower = [[None] * RANK for _ in range(RANK)]
        inverse = [None] * RANK
        for t in range(RANK):
            inverse[t] = 1.0 / pivot[t][t]
            for i in range(t + 1, RANK):
                lower[i][t] = pivot[i][t] * inverse[t]
            for i in range(t + 1, RANK):
                for j in range(t + 1, i + 1):
                    pivot[i][j] = pivot[i][j] - lower[i][t] * pivot[j][t]
                on_left[i] = on_left[i] - lower[i][t] * on_left[t]
                on_right[i] = on_right[i] - lower[i][t] * on_right[t]
        back_left, back_right = [None] * RANK, [None] * RANK
        for t in reversed(range(RANK)):
            back_left[t] = on_left[t] * inverse[t]
            back_right[t] = on_right[t] * inverse[t]
            for s in range(t + 1, RANK):
                back_left[t] = back_left[t] - lower[s][t] * back_left[s]
                back_right[t] = back_right[t] - lower[s][t] * back_right[s]
        for i in range(group, groups):
            if i == group and offset + RANK == 8:
                continue
            change_left = change_right = 0.0
            for t in range(RANK):
                if i == group:
                    factor = jnp.where(row >= offset + RANK, columns[t], 0.0)
                else:
                    factor = across_lanes(left[i], first + t)
                change_left = change_left + factor * back_left[t]
                change_right = change_right + factor * back_right[t]
            left[i] = left[i] - change_left
            right[i] = right[i] - change_right
        for t in range(RANK):
            scaled = on_right[t] * lax.rsqrt(pivot[t][t])
            finished[group] = jnp.where(row == offset + t, scaled, finished[group])
    return jnp.concatenate(finished, axis=0)


def factor_kernel(scale, gram_ref, tall_ref, solved_ref, lower_ref, work, factor):
    size = gram_ref.shape[0]
    work[:size, :] = gram_ref[...]
    work[size:, :] = tall_ref[...]

    def step(index, carry):
        columns = pl.ds(pl.multiple_of(index * BLOCK, BLOCK), BLOCK)
        inverse = inverse_factor(work[columns, columns])
        panel = lax.dot_general(
            work[:, columns],
            inverse,
            (((1,), (1,)), ((), ())),
            precision=HIGHEST,
            preferred_element_type=jnp.float32,
        )
        factor[:, columns] = panel

        @pl.when(index < size // BLOCK - 1)
        def _():
            work[...] -= lax.dot_general(
                panel,
                panel[:size],
                (((1,), (1,)), ((), ())),
                precision=HIGHEST,
                preferred_element_type=jnp.float32,
            )

        return carry

    lax.fori_loop(0, size // BLOCK, step, 0)
    solved_ref[...] = factor[size:, :]
    if lower_ref is not None:
        row = lax.broadcasted_iota(jnp.int32, (size, size), 0)
        column = lax.broadcasted_iota(jnp.int32, (size, size), 1)
        lower_ref[...] = jnp.where(row >= column, factor[:size, :] * scale, 0.0)


def factor_and_solve(gram, tall, scale=None):
    size, rows = gram.shape[0], tall.shape[0]
    shapes = [jax.ShapeDtypeStruct((rows, size), jnp.float32)]
    if scale is None:

        def body(gram_ref, tall_ref, solved_ref, work, factor):
            factor_kernel(None, gram_ref, tall_ref, solved_ref, None, work, factor)

    else:
        shapes.append(jax.ShapeDtypeStruct((size, size), jnp.float32))
        body = functools.partial(factor_kernel, scale)
    held = pltpu.VMEM((size + rows, size), jnp.float32)
    return pl.pallas_call(
        body,
        out_shape=shapes,
        in_specs=[pl.BlockSpec(memory_space=pltpu.VMEM)] * 2,
        out_specs=[pl.BlockSpec(memory_space=pltpu.VMEM)] * len(shapes),
        scratch_shapes=[held, held],
        compiler_params=pltpu.CompilerParams(vmem_limit_bytes=24 * 2**20),
        cost_estimate=pl.CostEstimate(
            flops=2 * size**3, bytes_accessed=8 * size * size, transcendentals=size
        ),
    )(gram, tall)


def gather(piece, axes):
    copies = jnp.broadcast_to(piece[None], (lax.axis_size(axes),) + piece.shape)
    return lax.all_to_all(copies, axes, 0, 0, tiled=True)


def gram_rows(left, right):
    return lax.dot_general(
        left,
        right,
        (((0,), (0,)), ((), ())),
        precision=HIGHEST,
        preferred_element_type=jnp.float32,
    )


def gather_gram(piece):
    size = piece.size
    eight = gather(piece, ("y", "col")).reshape(-1, size)
    four = gather(eight, ("x",)).reshape(-1, size)
    return gather(four, ("core",)).reshape(size, size)


def per_device(hidden_states, sketch_matrix):
    rows, block_width = hidden_states.shape
    size = sketch_matrix.shape[1]
    cols, spread = lax.axis_size("col"), lax.axis_size(ROW)
    total_rows, total_width = rows * spread, block_width * cols
    col = lax.axis_index("col")

    partial_sketch = jnp.dot(hidden_states, sketch_matrix, preferred_element_type=jnp.float32)
    parts = partial_sketch.reshape(cols, rows // cols, size)
    own = jnp.sum(lax.all_to_all(parts, "col", 0, 0, tiled=True), axis=0)
    sketch = gather(own, "col").reshape(rows, size)

    gram = gram_rows(sketch, sketch).reshape(size // cols, cols, size)
    share = lax.dynamic_index_in_dim(gram, col, 1, keepdims=False)
    share = lax.all_to_all(
        share.reshape(spread, 4, size // 4), ("core", "x", "y"), 0, 0, tiled=True
    )
    gram_left = gather_gram(jnp.sum(share, axis=0))
    (basis,) = factor_and_solve(gram_left, sketch)
    q_left = lax.dynamic_slice_in_dim(basis, col * (rows // cols), rows // cols, 0)
    q_left = q_left * math.sqrt(total_rows)

    image_rows = block_width // spread
    partial_image = lax.dot_general(
        hidden_states,
        basis.astype(jnp.bfloat16),
        (((0,), (0,)), ((), ())),
        preferred_element_type=jnp.float32,
    ).reshape(spread // 2, 2, image_rows, size)
    halves = jnp.sum(lax.all_to_all(partial_image, "core", 1, 1, tiled=True), axis=1)
    parts = lax.all_to_all(halves.astype(jnp.bfloat16), ("y", "x"), 0, 0, tiled=True)
    image = jnp.sum(parts.astype(jnp.float32), axis=0)

    near = gather(image, ("x", "core")).reshape(-1, size)
    start = (lax.axis_index("core") * 4 + lax.axis_index("x")) * (size // 8)
    chosen = lax.dynamic_slice_in_dim(near, start, size // 8, 1)
    share = gram_rows(chosen, near).reshape(size // 8, 4, size // 4)
    share = lax.all_to_all(share, ("y", "col"), 0, 0, tiled=True)
    gram_right = gather_gram(jnp.sum(share, axis=0))
    right, triangle = factor_and_solve(gram_right, image, 1.0 / math.sqrt(total_width))
    q_right = (right * math.sqrt(total_width)).reshape(1, image_rows, size)
    return (q_left, q_right, triangle)


def solution(mesh):
    fine = Mesh(mesh.devices.reshape(8, 4, 2, 8), ROW + ("col",))
    return jax.shard_map(
        per_device,
        mesh=fine,
        in_specs=(P(ROW, "col"), P("col", None)),
        out_specs=(P(ROW + ("col",), None), P("col", ROW, None), P()),
        check_vma=False,
    )
```

time: 1110 us -> 272 us (0.25)
  waiting for transfers between devices: 778 us -> 27.7 us
  other arithmetic: 252 us -> 3.39 us
  blocking collectives: 0 us -> 150 us
  Pallas kernels: 0 us -> 61.9 us
  matrix products: 27 us -> 4.79 us
  between operations: 19.7 us -> 0.81 us
  local copies, waits for them, and re-layouts: 26.6 us -> 9.28 us
  starting transfers between devices: 0.16 us -> 12.7 us
    psum x3 -> x0, waiting for transfers between devices: 638 us -> none  [the longest x1 279 us: per_device(): gram_left = lax.psum(gram_of(own_sketch), ('row', 'col'))]
    another operation x34 -> x0, other arithmetic: 249 us -> none  [the longest x29 158 us: factorize(): return jnp.linalg.cholesky(gram)]
    all_to_all x0 -> x10, blocking collectives: none -> 150 us  [the longest x5 57.3 us: gather(): return lax.all_to_all(copies, axes, 0, 0, tiled=True)]
    unnamed x5 -> x0, waiting for transfers between devices: 140 us -> none
    pallas_call x0 -> x2, Pallas kernels: none -> 61.9 us  [factor_and_solve(): pl.pallas_call(body, out_shape=shapes, in_specs=[pl.BlockSpec(memory_spac...]
    all_to_all x0 -> x3, waiting for transfers between devices: none -> 27.7 us  [gather(): return lax.all_to_all(copies, axes, 0, 0, tiled=True)]
    another operation x26 -> x0, matrix products: 17.5 us -> none  [the longest x12 10.9 us: factorize(): return jnp.linalg.cholesky(gram)]
    another operation x33 -> x0, local copies, waits for them, and re-layouts: 16.7 us -> none
  transfers between devices with their start and end apart: 4 -> 3, of which waited for: 4 -> 3; matrix products, arithmetic and copies ran while one was open for 0% -> 0% of each run, Pallas kernels for 0% -> 0%
where the time goes in v1:
time: 272 us; the launch traced here: 271 us
  blocking collectives  150 us (55%)
  Pallas kernels  61.9 us (23%)
  waiting for transfers between devices  27.7 us (10%)
  starting transfers between devices  12.7 us (5%)
  local copies, waits for them, and re-layouts  9.28 us (3%)
  matrix products  4.79 us (2%)
  other arithmetic  3.39 us (1%)
    pallas_call x2, Pallas kernels, factor_and_solve(): pl.pallas_call(body, out_shape=shapes, in_specs=[pl.BlockSpec(memory_spac...  61.9 us
    all_to_all x5, blocking collectives, gather(): return lax.all_to_all(copies, axes, 0, 0, tiled=True)  57.3 us
    all_to_all x3, waiting for transfers between devices, gather(): return lax.all_to_all(copies, axes, 0, 0, tiled=True)  27.7 us
    all_to_all x1, blocking collectives, per_device(): own = jnp.sum(lax.all_to_all(parts, 'col', 0, 0, tiled=True), axis=0)  26.7 us
    all_to_all x1, blocking collectives, per_device(): lax.all_to_all(share.reshape(spread, 4, size // 4), ('core', 'x', 'y'), 0...  24.2 us
    all_to_all x1, blocking collectives, per_device(): lax.all_to_all(halves.astype(jnp.bfloat16), ('y', 'x'), 0, 0, tiled=True)  20 us
    all_to_all x1, blocking collectives, per_device(): share = lax.all_to_all(share, ('y', 'col'), 0, 0, tiled=True)  15.9 us
    all_to_all x3, starting transfers between devices, gather(): return lax.all_to_all(copies, axes, 0, 0, tiled=True)  12.7 us
  transfers between devices with their start and end apart: 3, of which 3 were waited for; matrix products, arithmetic and copies ran while one was open for 0% of the time, Pallas kernels for 0%

profile of v1, /device:TPU:1, one launch (start us, length us, event | category | flops | bytes accessed | tf_op | source)
XLA Modules:
  0.0 270.9 jit_solution(11607993316757992584)
XLA Ops:
  0.6 0.0 copy-start
  0.6 1.2 copy-done
  1.9 1.5 fusion.7
  3.3 26.7 %all_to_all.65 = f32[8,32,512]{2,1,0:T(8,128)S(1)} all-to-all(f32[8,32,512]{2,1,0:T(8,128)S(1)} %bitcast.48), channel_id=1, replica_groups=mesh['y'=8,'x'=4,'core'=2,'col'=8] {'col'}, dimensions={0} | all-to-all | bytes 1048576 | tf_op jit(solution)/shard_map/all_to_all | solution.py:169
  30.0 0.9 broadcast_in_dim.24
  30.9 3.5 %all-to-all-start.1 = ((f32[8,32,512]{2,1,0:T(8,128)}), f32[8,32,512]{2,1,0:T(8,128)S(1)}, u32[]{:S(2)}, u32[]{:S(2)}) async-start(f32[8,32,512]{2,1,0:T(8,128)} %broadcast_in_dim.24), calls=%async_computation.1 | async-start | bytes 1048576 | tf_op jit(solution)/shard_map/all_to_all | solution.py:140
  34.4 14.9 %all-to-all-done.1 = f32[8,32,512]{2,1,0:T(8,128)S(1)} async-done(((f32[8,32,512]{2,1,0:T(8,128)}), f32[8,32,512]{2,1,0:T(8,128)S(1)}, u32[]{:S(2)}, u32[]{:S(2)}) %all-to-all-start.1) | async-done | bytes 524320 | tf_op jit(solution)/shard_map/all_to_all | solution.py:140
  49.3 0.2 copy.17
  49.5 1.0 fusion
  50.6 0.1 constant_dynamic-slice_fusion
  50.7 24.2 %all_to_all.66 = f32[64,4,128]{2,1,0:T(4,128)S(1)} all-to-all(f32[64,4,128]{2,1,0:T(4,128)S(1)} %bitcast.54), channel_id=1, replica_groups=mesh['y'=8,'x'=4,'core'=2,'col'=8] {'core','x','y'}, dimensions={0} | all-to-all | bytes 262144 | tf_op jit(solution)/shard_map/all_to_all | solution.py:174
  74.9 0.1 reduce_sum.46
  75.0 15.5 %all_to_all.67 = f32[64,4,128]{2,1,0:T(4,128)S(1)} all-to-all(f32[64,4,128]{2,1,0:T(4,128)S(1)} %broadcast_in_dim.25), channel_id=1, replica_groups=mesh['y'=8,'x'=4,'core'=2,'col'=8] {'y','col'}, dimensions={0} | all-to-all | bytes 262144 | tf_op jit(solution)/shard_map/all_to_all | solution.py:140
  90.5 0.1 broadcast_in_dim.27
  90.5 10.0 %all_to_all.68 = f32[4,64,512]{2,1,0:T(8,128)S(1)} all-to-all(f32[4,64,512]{2,1,0:T(8,128)S(1)} %broadcast_in_dim.27), channel_id=1, replica_groups=mesh['y'=8,'x'=4,'core'=2,'col'=8] {'x'}, dimensions={0} | all-to-all | bytes 1048576 | tf_op jit(solution)/shard_map/all_to_all | solution.py:140
  100.5 0.1 broadcast_in_dim.57
  100.7 0.0 copy-start.1
  100.7 7.5 %all_to_all.69 = f32[2,256,512]{2,1,0:T(8,128)S(1)} all-to-all(f32[2,256,512]{2,1,0:T(8,128)S(1)} %broadcast_in_dim.57), channel_id=1, replica_groups=mesh['y'=8,'x'=4,'core'=2,'col'=8] {'core'}, dimensions={0} | all-to-all | bytes 2097152 | tf_op jit(solution)/shard_map/all_to_all | solution.py:140
  108.2 31.2 %shard_map.49 = f32[256,512]{1,0:T(8,128)S(1)} custom-call(f32[512,512]{1,0:T(8,128)S(1)} %bitcast.44, f32[256,512]{1,0:T(8,128)S(1)} %bitcast.42), custom_call_target="tpu_custom_call" | custom-call | flops 268435456 | bytes 2097152 | tf_op jit(solution)/shard_map/pallas_call | solution.py:125
  139.4 0.0 copy-done.1
  139.4 1.8 convolution_bitcast_fusion
  141.2 2.9 %copy.18 = f32[1024,512]{1,0:T(8,128)} copy(f32[1024,512]{0,1:T(8,128)} %convolution_bitcast_fusion) | data formatting | bytes 4194304 | tf_op jit(solution)/shard_map/dot_general | solution.py:183
  144.1 1.8 copy.19
  146.0 6.3 %all_to_all.70 = f32[32,2,16,512]{3,2,0,1:T(8,128)} all-to-all(f32[32,2,16,512]{3,2,0,1:T(8,128)S(1)} %copy.19), channel_id=1, replica_groups=mesh['y'=8,'x'=4,'core'=2,'col'=8] {'core'}, dimensions={1} | all-to-all | bytes 4194304 | tf_op jit(solution)/shard_map/all_to_all | solution.py:189
  152.3 1.9 reduce_sum.47
  154.2 20.0 %all_to_all.71 = bf16[32,16,512]{2,1,0:T(8,128)(2,1)S(1)} all-to-all(bf16[32,16,512]{2,1,0:T(8,128)(2,1)S(1)} %reduce_sum.47), channel_id=1, replica_groups=mesh['y'=8,'x'=4,'core'=2,'col'=8] {'y','x'}, dimensions={0} | all-to-all | bytes 1048576 | tf_op jit(solution)/shard_map/all_to_all | solution.py:190
  174.2 0.1 convert_reduce_fusion.tall_ref
  174.2 0.7 broadcast_in_dim.58
  175.0 5.8 %all-to-all-start.8 = ((f32[8,16,512]{2,1,0:T(8,128)}), f32[8,16,512]{2,1,0:T(8,128)S(1)}, u32[]{:S(2)}, u32[]{:S(2)}) async-start(f32[8,16,512]{2,1,0:T(8,128)} %broadcast_in_dim.58), calls=%async_computation.8 | async-start | bytes 524288 | tf_op jit(solution)/shard_map/all_to_all | solution.py:140
  180.7 6.5 %all-to-all-done.8 = f32[8,16,512]{2,1,0:T(8,128)S(1)} async-done(((f32[8,16,512]{2,1,0:T(8,128)}), f32[8,16,512]{2,1,0:T(8,128)S(1)}, u32[]{:S(2)}, u32[]{:S(2)}) %all-to-all-start.8) | async-done | bytes 262176 | tf_op jit(solution)/shard_map/all_to_all | solution.py:140
  187.3 0.1 copy.21
  187.4 0.5 fusion.3
  187.9 0.1 copy.22
  188.0 15.9 %all_to_all.72 = f32[64,4,128]{2,1,0:T(4,128)S(1)} all-to-all(f32[64,4,128]{2,1,0:T(4,128)S(1)} %copy.22), channel_id=1, replica_groups=mesh['y'=8,'x'=4,'core'=2,'col'=8] {'y','col'}, dimensions={0} | all-to-all | bytes 262144 | tf_op jit(solution)/shard_map/all_to_all | solution.py:197
  203.8 0.1 reduce_sum.49
  203.9 15.4 %all_to_all.73 = f32[64,4,128]{2,1,0:T(4,128)S(1)} all-to-all(f32[64,4,128]{2,1,0:T(4,128)S(1)} %broadcast_in_dim.59), channel_id=1, replica_groups=mesh['y'=8,'x'=4,'core'=2,'col'=8] {'y','col'}, dimensions={0} | all-to-all | bytes 262144 | tf_op jit(solution)/shard_map/all_to_all | solution.py:140
  219.4 0.9 broadcast_in_dim.61
  220.2 3.5 %all-to-all-start.11 = ((f32[4,64,512]{2,1,0:T(8,128)}), f32[4,64,512]{2,1,0:T(8,128)S(1)}, u32[]{:S(2)}, u32[]{:S(2)}) async-start(f32[4,64,512]{2,1,0:T(8,128)} %broadcast_in_dim.61), calls=%async_computation.11 | async-start | bytes 1048576 | tf_op jit(solution)/shard_map/all_to_all | solution.py:140
  223.7 0.6 dynamic-slice_multiply_fusion
  224.4 6.3 %all-to-all-done.11 = f32[4,64,512]{2,1,0:T(8,128)S(1)} async-done(((f32[4,64,512]{2,1,0:T(8,128)}), f32[4,64,512]{2,1,0:T(8,128)S(1)}, u32[]{:S(2)}, u32[]{:S(2)}) %all-to-all-start.11) | async-done | bytes 524320 | tf_op jit(solution)/shard_map/all_to_all | solution.py:140
  230.6 0.1 broadcast_in_dim.63
  230.7 8.9 %all_to_all.74 = f32[2,256,512]{2,1,0:T(8,128)S(1)} all-to-all(f32[2,256,512]{2,1,0:T(8,128)S(1)} %broadcast_in_dim.63), channel_id=1, replica_groups=mesh['y'=8,'x'=4,'core'=2,'col'=8] {'core'}, dimensions={0} | all-to-all | bytes 2097152 | tf_op jit(solution)/shard_map/all_to_all | solution.py:140
  239.6 30.7 %shard_map.50 = (f32[16,512]{1,0:T(8,128)S(1)}, f32[512,512]{1,0:T(8,128)}) custom-call(f32[512,512]{1,0:T(8,128)S(1)} %bitcast.43, f32[16,512]{1,0:T(8,128)S(1)} %convert_reduce_fusion.tall_ref), custom_call_target="tpu_custom_call" | custom-call | flops 268435456 | bytes 2097152 | tf_op jit(solution)/shard_map/pallas_call | solution.py:125
  270.3 0.6 multiply_bitcast_fusion
  (5 shorter events, 0.1 us)
Async XLA Ops:
  0.6 1.2 copy-start
  30.9 18.4 %all-to-all-start.1 = ((f32[8,32,512]{2,1,0:T(8,128)}), f32[8,32,512]{2,1,0:T(8,128)S(1)}, u32[]{:S(2)}, u32[]{:S(2)}) async-start(f32[8,32,512]{2,1,0:T(8,128)} %broadcast_in_dim.24), calls=%async_computation.1 | async-start | bytes 1048576 | tf_op jit(solution)/shard_map/all_to_all | solution.py:140
  100.7 38.8 %copy-start.1 = (bf16[256,1024]{1,0:T(8,128)(2,1)S(1)}, bf16[256,1024]{1,0:T(8,128)(2,1)}, u32[]{:S(2)}) copy-start(bf16[256,1024]{1,0:T(8,128)(2,1)} %param.2) | copy-start | bytes 1572868
  175.0 12.3 %all-to-all-start.8 = ((f32[8,16,512]{2,1,0:T(8,128)}), f32[8,16,512]{2,1,0:T(8,128)S(1)}, u32[]{:S(2)}, u32[]{:S(2)}) async-start(f32[8,16,512]{2,1,0:T(8,128)} %broadcast_in_dim.58), calls=%async_computation.8 | async-start | bytes 524288 | tf_op jit(solution)/shard_map/all_to_all | solution.py:140
  220.2 10.4 %all-to-all-start.11 = ((f32[4,64,512]{2,1,0:T(8,128)}), f32[4,64,512]{2,1,0:T(8,128)S(1)}, u32[]{:S(2)}, u32[]{:S(2)}) async-start(f32[4,64,512]{2,1,0:T(8,128)} %broadcast_in_dim.61), calls=%async_computation.11 | async-start | bytes 1048576 | tf_op jit(solution)/shard_map/all_to_all | solution.py:140

commit v2 on v1

--- a/solution.py
+++ b/solution.py
@@ -16,7 +16,8 @@
 
 
 def across_lanes(piece, column):
-    return jnp.broadcast_to(piece[:, column : column + 1], piece.shape)
+    place = jnp.full(piece.shape, column, jnp.int32)
+    return jnp.take_along_axis(piece, place, axis=1, mode="promise_in_bounds")
 
 
 def across_rows(piece, row):
@@ -51,88 +52,98 @@
         for t in reversed(range(RANK)):
             back_left[t] = on_left[t] * inverse[t]
             back_right[t] = on_right[t] * inverse[t]
-            for s in range(t + 1, RANK):
+            for s in reversed(range(t + 1, RANK)):
                 back_left[t] = back_left[t] - lower[s][t] * back_left[s]
                 back_right[t] = back_right[t] - lower[s][t] * back_right[s]
         for i in range(group, groups):
             if i == group and offset + RANK == 8:
                 continue
-            change_left = change_right = 0.0
-            for t in range(RANK):
+            new_left, new_right = left[i], right[i]
+            for t in reversed(range(RANK)):
                 if i == group:
                     factor = jnp.where(row >= offset + RANK, columns[t], 0.0)
                 else:
                     factor = across_lanes(left[i], first + t)
-                change_left = change_left + factor * back_left[t]
-                change_right = change_right + factor * back_right[t]
-            left[i] = left[i] - change_left
-            right[i] = right[i] - change_right
+                new_left = new_left - factor * back_left[t]
+                new_right = new_right - factor * back_right[t]
+            left[i], right[i] = new_left, new_right
         for t in range(RANK):
             scaled = on_right[t] * lax.rsqrt(pivot[t][t])
             finished[group] = jnp.where(row == offset + t, scaled, finished[group])
     return jnp.concatenate(finished, axis=0)
 
 
-def factor_kernel(scale, gram_ref, tall_ref, solved_ref, lower_ref, work, factor):
+def times_transposed(left, right):
+    return lax.dot_general(
+        left,
+        right,
+        (((1,), (1,)), ((), ())),
+        precision=HIGHEST,
+        preferred_element_type=jnp.float32,
+    )
+
+
+def factor_blocks(gram_ref, tall_ref, work, factor, inverse):
     size = gram_ref.shape[0]
     work[:size, :] = gram_ref[...]
     work[size:, :] = tall_ref[...]
 
     def step(index, carry):
-        columns = pl.ds(pl.multiple_of(index * BLOCK, BLOCK), BLOCK)
-        inverse = inverse_factor(work[columns, columns])
-        panel = lax.dot_general(
-            work[:, columns],
-            inverse,
-            (((1,), (1,)), ((), ())),
-            precision=HIGHEST,
-            preferred_element_type=jnp.float32,
-        )
-        factor[:, columns] = panel
-
-        @pl.when(index < size // BLOCK - 1)
-        def _():
-            work[...] -= lax.dot_general(
-                panel,
-                panel[:size],
-                (((1,), (1,)), ((), ())),
-                precision=HIGHEST,
-                preferred_element_type=jnp.float32,
-            )
+        here = pl.ds(pl.multiple_of(index * BLOCK, BLOCK), BLOCK)
+        inverse[...] = inverse_factor(work[here, here])
+        for block in range(size // BLOCK):
+            first, after = block * BLOCK, (block + 1) * BLOCK
+
+            @pl.when(index == block)
+            def _(first=first, after=after):
+                panel = times_transposed(work[first:, first:after], inverse[...])
+                factor[first:, first:after] = panel
+                if after < size:
+                    below, right = panel[BLOCK:], panel[BLOCK : size - first]
+                    work[after:, after:] -= times_transposed(below, right)
 
         return carry
 
     lax.fori_loop(0, size // BLOCK, step, 0)
-    solved_ref[...] = factor[size:, :]
-    if lower_ref is not None:
-        row = lax.broadcasted_iota(jnp.int32, (size, size), 0)
-        column = lax.broadcasted_iota(jnp.int32, (size, size), 1)
-        lower_ref[...] = jnp.where(row >= column, factor[:size, :] * scale, 0.0)
-
-
-def factor_and_solve(gram, tall, scale=None):
-    size, rows = gram.shape[0], tall.shape[0]
-    shapes = [jax.ShapeDtypeStruct((rows, size), jnp.float32)]
-    if scale is None:
-
-        def body(gram_ref, tall_ref, solved_ref, work, factor):
-            factor_kernel(None, gram_ref, tall_ref, solved_ref, None, work, factor)
-
-    else:
-        shapes.append(jax.ShapeDtypeStruct((size, size), jnp.float32))
-        body = functools.partial(factor_kernel, scale)
+
+
+def left_kernel(gram_ref, tall_ref, turned_ref, solved_ref, image_ref, work, factor, inverse):
+    size = gram_ref.shape[0]
+    factor_blocks(gram_ref, tall_ref, work, factor, inverse)
+    basis = factor[size:, :]
+    solved_ref[...] = basis
+    image = jnp.dot(
+        turned_ref[...], basis.astype(jnp.bfloat16), preferred_element_type=jnp.float32
+    )
+    halves, rows, _ = image_ref.shape
+    image = image.reshape(rows // 16, halves, 16, size)
+    for half in range(halves):
+        image_ref[half] = image[:, half].reshape(rows, size)
+
+
+def right_kernel(scales, gram_ref, tall_ref, solved_ref, lower_ref, work, factor, inverse):
+    size = gram_ref.shape[0]
+    factor_blocks(gram_ref, tall_ref, work, factor, inverse)
+    solved_ref[...] = factor[size:, :] * scales[0]
+    row = lax.broadcasted_iota(jnp.int32, (size, size), 0)
+    column = lax.broadcasted_iota(jnp.int32, (size, size), 1)
+    lower_ref[...] = jnp.where(row >= column, factor[:size, :] * scales[1], 0.0)
+
+
+def call_factor(kernel, shapes, operands):
+    size, rows = operands[0].shape[0], operands[1].shape[0]
     held = pltpu.VMEM((size + rows, size), jnp.float32)
     return pl.pallas_call(
-        body,
-        out_shape=shapes,
-        in_specs=[pl.BlockSpec(memory_space=pltpu.VMEM)] * 2,
+        kernel,
+        out_shape=[jax.ShapeDtypeStruct(shape, jnp.float32) for shape in shapes],
+        in_specs=[pl.BlockSpec(memory_space=pltpu.VMEM)] * len(operands),
         out_specs=[pl.BlockSpec(memory_space=pltpu.VMEM)] * len(shapes),
-        scratch_shapes=[held, held],
-        compiler_params=pltpu.CompilerParams(vmem_limit_bytes=24 * 2**20),
+        scratch_shapes=[held, held, pltpu.VMEM((BLOCK, BLOCK), jnp.float32)],
+        compiler_params=pltpu.CompilerParams(vmem_limit_bytes=32 * 2**20),
         cost_estimate=pl.CostEstimate(
             flops=2 * size**3, bytes_accessed=8 * size * size, transcendentals=size
         ),
-    )(gram, tall)
+    )(*operands)
 
 
 def gather(piece, axes):
@@ -175,19 +186,18 @@
         share.reshape(spread, 4, size // 4), ("core", "x", "y"), 0, 0, tiled=True
     )
     gram_left = gather_gram(jnp.sum(share, axis=0))
-    (basis,) = factor_and_solve(gram_left, sketch)
+    image_rows = block_width // spread
+    basis, partial_image = call_factor(
+        left_kernel,
+        [(rows, size), (2, block_width // 2, size)],
+        [gram_left, sketch, hidden_states.T],
+    )
     q_left = lax.dynamic_slice_in_dim(basis, col * (rows // cols), rows // cols, 0)
     q_left = q_left * math.sqrt(total_rows)
 
-    image_rows = block_width // spread
-    partial_image = lax.dot_general(
-        hidden_states,
-        basis.astype(jnp.bfloat16),
-        (((0,), (0,)), ((), ())),
-        preferred_element_type=jnp.float32,
-    ).reshape(spread // 2, 2, image_rows, size)
-    halves = jnp.sum(lax.all_to_all(partial_image, "core", 1, 1, tiled=True), axis=1)
-    parts = lax.all_to_all(halves.astype(jnp.bfloat16), ("y", "x"), 0, 0, tiled=True)
+    halves = jnp.sum(lax.all_to_all(partial_image, "core", 0, 0, tiled=True), axis=0)
+    parts = halves.astype(jnp.bfloat16).reshape(spread // 2, image_rows, size)
+    parts = lax.all_to_all(parts, ("y", "x"), 0, 0, tiled=True)
     image = jnp.sum(parts.astype(jnp.float32), axis=0)
 
     near = gather(image, ("x", "core")).reshape(-1, size)
@@ -196,9 +206,13 @@
     share = gram_rows(chosen, near).reshape(size // 8, 4, size // 4)
     share = lax.all_to_all(share, ("y", "col"), 0, 0, tiled=True)
     gram_right = gather_gram(jnp.sum(share, axis=0))
-    right, triangle = factor_and_solve(gram_right, image, 1.0 / math.sqrt(total_width))
-    q_right = (right * math.sqrt(total_width)).reshape(1, image_rows, size)
-    return (q_left, q_right, triangle)
+    scales = (math.sqrt(total_width), 1.0 / math.sqrt(total_width))
+    q_right, triangle = call_factor(
+        functools.partial(right_kernel, scales),
+        [(image_rows, size), (size, size)],
+        [gram_right, image],
+    )
+    return (q_left, q_right.reshape(1, image_rows, size), triangle)
 
 
 def solution(mesh):

time: 272 us -> 239 us (0.88)
  Pallas kernels: 61.9 us -> 35.3 us
  blocking collectives: 150 us -> 140 us
  waiting for transfers between devices: 27.7 us -> 34.4 us
  local copies, waits for them, and re-layouts: 9.28 us -> 5.54 us
  starting transfers between devices: 12.7 us -> 16.2 us
    pallas_call x2, Pallas kernels: 61.9 us -> 35.3 us  [call_factor(): pl.pallas_call(kernel, out_shape=[jax.ShapeDtypeStruct(shape, jnp.float32...]
    all_to_all x5 -> x4, blocking collectives: 57.3 us -> 47.4 us  [gather(): return lax.all_to_all(copies, axes, 0, 0, tiled=True)]
    all_to_all x3 -> x4, waiting for transfers between devices: 27.7 us -> 34.4 us  [gather(): return lax.all_to_all(copies, axes, 0, 0, tiled=True)]
    all_to_all x3 -> x4, starting transfers between devices: 12.7 us -> 16.2 us  [gather(): return lax.all_to_all(copies, axes, 0, 0, tiled=True)]
    dot_general x1 -> x0, local copies, waits for them, and re-layouts: 2.89 us -> none  [per_device(): lax.dot_general(hidden_states, basis.astype(jnp.bfloat16), (((0,), (0,)),...]
  transfers between devices with their start and end apart: 3 -> 4, of which waited for: 3 -> 4; matrix products, arithmetic and copies ran while one was open for 0% -> 0% of each run, Pallas kernels for 0% -> 0%
where the time goes in v2:
time: 239 us; the launch traced here: 238 us
  blocking collectives  140 us (59%)
  Pallas kernels  35.3 us (15%)
  waiting for transfers between devices  34.4 us (14%)
  starting transfers between devices  16.2 us (7%)
  local copies, waits for them, and re-layouts  5.54 us (2%)
  matrix products  2.97 us (1%)
  other arithmetic  2.76 us (1%)
    all_to_all x4, blocking collectives, gather(): return lax.all_to_all(copies, axes, 0, 0, tiled=True)  47.4 us
    pallas_call x2, Pallas kernels, call_factor(): pl.pallas_call(kernel, out_shape=[jax.ShapeDtypeStruct(shape, jnp.float32...  35.3 us
    all_to_all x4, waiting for transfers between devices, gather(): return lax.all_to_all(copies, axes, 0, 0, tiled=True)  34.4 us
    all_to_all x1, blocking collectives, per_device(): own = jnp.sum(lax.all_to_all(parts, 'col', 0, 0, tiled=True), axis=0)  26.7 us
    all_to_all x1, blocking collectives, per_device(): lax.all_to_all(share.reshape(spread, 4, size // 4), ('core', 'x', 'y'), 0...  24.2 us
    all_to_all x1, blocking collectives, per_device(): parts = lax.all_to_all(parts, ('y', 'x'), 0, 0, tiled=True)  19.6 us
    all_to_all x4, starting transfers between devices, gather(): return lax.all_to_all(copies, axes, 0, 0, tiled=True)  16.2 us
    all_to_all x1, blocking collectives, per_device(): share = lax.all_to_all(share, ('y', 'col'), 0, 0, tiled=True)  15.9 us
  transfers between devices with their start and end apart: 4, of which 4 were waited for; matrix products, arithmetic and copies ran while one was open for 0% of the time, Pallas kernels for 0%

profile of v2, /device:TPU:1, one launch (start us, length us, event | category | flops | bytes accessed | tf_op | source)
XLA Modules:
  0.0 238.1 jit_solution(3966461227128077077)
XLA Ops:
  0.6 0.0 copy-start
  0.6 1.2 copy-done
  1.9 1.5 fusion.6
  3.3 26.7 %all_to_all.65 = f32[8,32,512]{2,1,0:T(8,128)S(1)} all-to-all(f32[8,32,512]{2,1,0:T(8,128)S(1)} %bitcast.46), channel_id=1, replica_groups=mesh['y'=8,'x'=4,'core'=2,'col'=8] {'col'}, dimensions={0} | all-to-all | bytes 1048576 | tf_op jit(solution)/shard_map/all_to_all | solution.py:180
  30.0 0.9 broadcast_in_dim.24
  30.9 3.5 %all-to-all-start.1 = ((f32[8,32,512]{2,1,0:T(8,128)}), f32[8,32,512]{2,1,0:T(8,128)S(1)}, u32[]{:S(2)}, u32[]{:S(2)}) async-start(f32[8,32,512]{2,1,0:T(8,128)} %broadcast_in_dim.24), calls=%async_computation.1 | async-start | bytes 1048576 | tf_op jit(solution)/shard_map/all_to_all | solution.py:151
  34.4 14.9 %all-to-all-done.1 = f32[8,32,512]{2,1,0:T(8,128)S(1)} async-done(((f32[8,32,512]{2,1,0:T(8,128)}), f32[8,32,512]{2,1,0:T(8,128)S(1)}, u32[]{:S(2)}, u32[]{:S(2)}) %all-to-all-start.1) | async-done | bytes 524320 | tf_op jit(solution)/shard_map/all_to_all | solution.py:151
  49.3 0.2 copy.17
  49.5 0.0 copy-start.1
  49.5 1.0 fusion
  50.6 0.1 constant_dynamic-slice_fusion
  50.7 24.2 %all_to_all.66 = f32[64,4,128]{2,1,0:T(4,128)S(1)} all-to-all(f32[64,4,128]{2,1,0:T(4,128)S(1)} %bitcast.52), channel_id=1, replica_groups=mesh['y'=8,'x'=4,'core'=2,'col'=8] {'core','x','y'}, dimensions={0} | all-to-all | bytes 262144 | tf_op jit(solution)/shard_map/all_to_all | solution.py:185
  74.9 0.1 reduce_sum.46
  75.0 15.5 %all_to_all.67 = f32[64,4,128]{2,1,0:T(4,128)S(1)} all-to-all(f32[64,4,128]{2,1,0:T(4,128)S(1)} %broadcast_in_dim.25), channel_id=1, replica_groups=mesh['y'=8,'x'=4,'core'=2,'col'=8] {'y','col'}, dimensions={0} | all-to-all | bytes 262144 | tf_op jit(solution)/shard_map/all_to_all | solution.py:151
  90.5 0.9 broadcast_in_dim.27
  91.3 3.5 %all-to-all-start.4 = ((f32[4,64,512]{2,1,0:T(8,128)}), f32[4,64,512]{2,1,0:T(8,128)S(1)}, u32[]{:S(2)}, u32[]{:S(2)}) async-start(f32[4,64,512]{2,1,0:T(8,128)} %broadcast_in_dim.27), calls=%async_computation.4 | async-start | bytes 1048576 | tf_op jit(solution)/shard_map/all_to_all | solution.py:151
  94.8 0.0 copy-done.1
  94.8 0.2 copy.18
  95.0 6.7 %all-to-all-done.4 = f32[4,64,512]{2,1,0:T(8,128)S(1)} async-done(((f32[4,64,512]{2,1,0:T(8,128)}), f32[4,64,512]{2,1,0:T(8,128)S(1)}, u32[]{:S(2)}, u32[]{:S(2)}) %all-to-all-start.4) | async-done | bytes 524320 | tf_op jit(solution)/shard_map/all_to_all | solution.py:151
  101.7 0.1 broadcast_in_dim.57
  101.9 7.7 %all_to_all.68 = f32[2,256,512]{2,1,0:T(8,128)S(1)} all-to-all(f32[2,256,512]{2,1,0:T(8,128)S(1)} %broadcast_in_dim.57), channel_id=1, replica_groups=mesh['y'=8,'x'=4,'core'=2,'col'=8] {'core'}, dimensions={0} | all-to-all | bytes 2097152 | tf_op jit(solution)/shard_map/all_to_all | solution.py:151
  109.5 17.9 %shard_map.49 = (f32[256,512]{1,0:T(8,128)S(1)}, f32[2,512,512]{2,1,0:T(8,128)S(1)}) custom-call(f32[512,512]{1,0:T(8,128)S(1)} %bitcast.40, f32[256,512]{1,0:T(8,128)S(1)} %bitcast.39, bf16[1024,256]{1,0:T(8,128)(2,1)S(1)} %bitcast.42), custom_call_target="tpu_custom_call" | custom-call | flops 268435456 | bytes 2097152 | tf_op jit(solution)/shard_map/pallas_call | solution.py:136
  127.5 6.3 %all_to_all.69 = f32[2,512,512]{2,1,0:T(8,128)} all-to-all(f32[2,512,512]{2,1,0:T(8,128)S(1)} %get-tuple-element.8), channel_id=1, replica_groups=mesh['y'=8,'x'=4,'core'=2,'col'=8] {'core'}, dimensions={0} | all-to-all | bytes 4194304 | tf_op jit(solution)/shard_map/all_to_all | solution.py:198
  133.8 1.8 reduce_sum.47
  135.6 19.6 %all_to_all.70 = bf16[32,16,512]{2,1,0:T(8,128)(2,1)S(1)} all-to-all(bf16[32,16,512]{2,1,0:T(8,128)(2,1)S(1)} %bitcast.45), channel_id=1, replica_groups=mesh['y'=8,'x'=4,'core'=2,'col'=8] {'y','x'}, dimensions={0} | all-to-all | bytes 1048576 | tf_op jit(solution)/shard_map/all_to_all | solution.py:200
  155.3 0.1 convert_reduce_fusion.tall_ref
  155.3 0.7 broadcast_in_dim.58
  156.1 5.8 %all-to-all-start.8 = ((f32[8,16,512]{2,1,0:T(8,128)}), f32[8,16,512]{2,1,0:T(8,128)S(1)}, u32[]{:S(2)}, u32[]{:S(2)}) async-start(f32[8,16,512]{2,1,0:T(8,128)} %broadcast_in_dim.58), calls=%async_computation.8 | async-start | bytes 524288 | tf_op jit(solution)/shard_map/all_to_all | solution.py:151
  161.8 6.5 %all-to-all-done.8 = f32[8,16,512]{2,1,0:T(8,128)S(1)} async-done(((f32[8,16,512]{2,1,0:T(8,128)}), f32[8,16,512]{2,1,0:T(8,128)S(1)}, u32[]{:S(2)}, u32[]{:S(2)}) %all-to-all-start.8) | async-done | bytes 262176 | tf_op jit(solution)/shard_map/all_to_all | solution.py:151
  168.4 0.1 copy.20
  168.5 0.5 fusion.2
  169.0 0.1 copy.21
  169.1 15.9 %all_to_all.71 = f32[64,4,128]{2,1,0:T(4,128)S(1)} all-to-all(f32[64,4,128]{2,1,0:T(4,128)S(1)} %copy.21), channel_id=1, replica_groups=mesh['y'=8,'x'=4,'core'=2,'col'=8] {'y','col'}, dimensions={0} | all-to-all | bytes 262144 | tf_op jit(solution)/shard_map/all_to_all | solution.py:207
  185.0 0.1 reduce_sum.49
  185.1 15.4 %all_to_all.72 = f32[64,4,128]{2,1,0:T(4,128)S(1)} all-to-all(f32[64,4,128]{2,1,0:T(4,128)S(1)} %broadcast_in_dim.59), channel_id=1, replica_groups=mesh['y'=8,'x'=4,'core'=2,'col'=8] {'y','col'}, dimensions={0} | all-to-all | bytes 262144 | tf_op jit(solution)/shard_map/all_to_all | solution.py:151
  200.5 0.9 broadcast_in_dim.61
  201.4 3.5 %all-to-all-start.11 = ((f32[4,64,512]{2,1,0:T(8,128)}), f32[4,64,512]{2,1,0:T(8,128)S(1)}, u32[]{:S(2)}, u32[]{:S(2)}) async-start(f32[4,64,512]{2,1,0:T(8,128)} %broadcast_in_dim.61), calls=%async_computation.11 | async-start | bytes 1048576 | tf_op jit(solution)/shard_map/all_to_all | solution.py:151
  204.9 0.6 dynamic-slice_multiply_fusion
  205.5 6.3 %all-to-all-done.11 = f32[4,64,512]{2,1,0:T(8,128)S(1)} async-done(((f32[4,64,512]{2,1,0:T(8,128)}), f32[4,64,512]{2,1,0:T(8,128)S(1)}, u32[]{:S(2)}, u32[]{:S(2)}) %all-to-all-start.11) | async-done | bytes 524320 | tf_op jit(solution)/shard_map/all_to_all | solution.py:151
  211.8 0.1 broadcast_in_dim.63
  211.9 8.9 %all_to_all.73 = f32[2,256,512]{2,1,0:T(8,128)S(1)} all-to-all(f32[2,256,512]{2,1,0:T(8,128)S(1)} %broadcast_in_dim.63), channel_id=1, replica_groups=mesh['y'=8,'x'=4,'core'=2,'col'=8] {'core'}, dimensions={0} | all-to-all | bytes 2097152 | tf_op jit(solution)/shard_map/all_to_all | solution.py:151
  220.8 17.4 %shard_map.50 = (f32[16,512]{1,0:T(8,128)}, f32[512,512]{1,0:T(8,128)}) custom-call(f32[512,512]{1,0:T(8,128)S(1)} %bitcast.41, f32[16,512]{1,0:T(8,128)S(1)} %convert_reduce_fusion.tall_ref), custom_call_target="tpu_custom_call" | custom-call | flops 268435456 | bytes 2097152 | tf_op jit(solution)/shard_map/pallas_call | solution.py:136
  (5 shorter events, 0.1 us)
Async XLA Ops:
  0.6 1.2 copy-start
  30.9 18.4 %all-to-all-start.1 = ((f32[8,32,512]{2,1,0:T(8,128)}), f32[8,32,512]{2,1,0:T(8,128)S(1)}, u32[]{:S(2)}, u32[]{:S(2)}) async-start(f32[8,32,512]{2,1,0:T(8,128)} %broadcast_in_dim.24), calls=%async_computation.1 | async-start | bytes 1048576 | tf_op jit(solution)/shard_map/all_to_all | solution.py:151
  49.5 45.3 %copy-start.1 = (bf16[256,1024]{1,0:T(8,128)(2,1)S(1)}, bf16[256,1024]{1,0:T(8,128)(2,1)}, u32[]{:S(2)}) copy-start(bf16[256,1024]{1,0:T(8,128)(2,1)} %param.2) | copy-start | bytes 1572868
  91.3 10.4 %all-to-all-start.4 = ((f32[4,64,512]{2,1,0:T(8,128)}), f32[4,64,512]{2,1,0:T(8,128)S(1)}, u32[]{:S(2)}, u32[]{:S(2)}) async-start(f32[4,64,512]{2,1,0:T(8,128)} %broadcast_in_dim.27), calls=%async_computation.4 | async-start | bytes 1048576 | tf_op jit(solution)/shard_map/all_to_all | solution.py:151
  156.1 12.3 %all-to-all-start.8 = ((f32[8,16,512]{2,1,0:T(8,128)}), f32[8,16,512]{2,1,0:T(8,128)S(1)}, u32[]{:S(2)}, u32[]{:S(2)}) async-start(f32[8,16,512]{2,1,0:T(8,128)} %broadcast_in_dim.58), calls=%async_computation.8 | async-start | bytes 524288 | tf_op jit(solution)/shard_map/all_to_all | solution.py:151
  201.4 10.4 %all-to-all-start.11 = ((f32[4,64,512]{2,1,0:T(8,128)}), f32[4,64,512]{2,1,0:T(8,128)S(1)}, u32[]{:S(2)}, u32[]{:S(2)}) async-start(f32[4,64,512]{2,1,0:T(8,128)} %broadcast_in_dim.61), calls=%async_computation.11 | async-start | bytes 1048576 | tf_op jit(solution)/shard_map/all_to_all | solution.py:151

commit v3 on v2

--- a/solution.py
+++ b/solution.py
@@ -85,7 +85,6 @@
 
 def factor_blocks(gram_ref, tall_ref, work, factor, inverse):
     size = gram_ref.shape[0]
-    work[:size, :] = gram_ref[...]
     work[size:, :] = tall_ref[...]
 
     def step(index, carry):
@@ -109,6 +108,10 @@
 
 def left_kernel(gram_ref, tall_ref, turned_ref, solved_ref, image_ref, work, factor, inverse):
     size = gram_ref.shape[0]
+    for place in range(size // 8):
+        y, x, core = place // 8, place // 2 % 4, place % 2
+        came = (core * 4 + x) * 8 + y
+        work[8 * place : 8 * place + 8, :] = gram_ref[8 * came : 8 * came + 8, :]
     factor_blocks(gram_ref, tall_ref, work, factor, inverse)
     basis = factor[size:, :]
     solved_ref[...] = basis
@@ -123,6 +126,7 @@
 
 def right_kernel(scales, gram_ref, tall_ref, solved_ref, lower_ref, work, factor, inverse):
     size = gram_ref.shape[0]
+    work[:size, :] = gram_ref[...]
     factor_blocks(gram_ref, tall_ref, work, factor, inverse)
     solved_ref[...] = factor[size:, :] * scales[0]
     row = lax.broadcasted_iota(jnp.int32, (size, size), 0)
@@ -151,6 +155,19 @@
     return lax.all_to_all(copies, axes, 0, 0, tiled=True)
 
 
+def pack(values):
+    power = jnp.clip(jnp.ceil(jnp.log2(jnp.max(jnp.abs(values)))), -100.0, 100.0)
+    scaled = (values * jnp.exp2(14.0 - power)).astype(jnp.float16)
+    lanes = jnp.full((*values.shape[:-1], 128), power, jnp.float16)
+    return jnp.concatenate([scaled, lanes], axis=-1)
+
+
+def unpack(message):
+    size = message.shape[-1] - 128
+    power = message[..., size : size + 1].astype(jnp.float32)
+    return message[..., :size].astype(jnp.float32) * jnp.exp2(power - 14.0)
+
+
 def gram_rows(left, right):
     return lax.dot_general(
         left,
@@ -176,15 +193,13 @@
     col = lax.axis_index("col")
 
     partial_sketch = jnp.dot(hidden_states, sketch_matrix, preferred_element_type=jnp.float32)
-    parts = partial_sketch.reshape(cols, rows // cols, size)
-    own = jnp.sum(lax.all_to_all(parts, "col", 0, 0, tiled=True), axis=0)
-    sketch = gather(own, "col").reshape(rows, size)
+    parts = pack(partial_sketch).reshape(cols, rows // cols, size + 128)
+    own = jnp.sum(unpack(lax.all_to_all(parts, "col", 0, 0, tiled=True)), axis=0)
+    sketch = unpack(gather(pack(own), "col")).reshape(rows, size)
 
     gram = gram_rows(sketch, sketch).reshape(size // cols, cols, size)
     share = lax.dynamic_index_in_dim(gram, col, 1, keepdims=False)
-    share = lax.all_to_all(
-        share.reshape(spread, 4, size // 4), ("core", "x", "y"), 0, 0, tiled=True
-    )
+    share = lax.all_to_all(share.reshape(spread, 4, size // 4), ROW, 0, 0, tiled=True)
     gram_left = gather_gram(jnp.sum(share, axis=0))
     image_rows = block_width // spread
     basis, partial_image = call_factor(

time: 239 us -> 234 us (0.979)
  waiting for transfers between devices: 34.4 us -> 29.4 us
  blocking collectives: 140 us -> 137 us
    all_to_all x4, waiting for transfers between devices: 34.4 us -> 29.4 us  [gather(): return lax.all_to_all(copies, axes, 0, 0, tiled=True)]
    all_to_all x2, blocking collectives: 50.8 us -> 47.6 us  [the longest x1 25.3 us: per_device(): lax.all_to_all(share.reshape(spread, 4, size // 4), ROW, 0, 0, tiled=True)]
where the time goes in v3:
time: 234 us; the launch traced here: 233 us
  blocking collectives  137 us (59%)
  Pallas kernels  35.3 us (15%)
  waiting for transfers between devices  29.4 us (13%)
  starting transfers between devices  16.1 us (7%)
  local copies, waits for them, and re-layouts  5.79 us (2%)
  other arithmetic  3.66 us (2%)
  matrix products  3.61 us (2%)
    all_to_all x4, blocking collectives, gather(): return lax.all_to_all(copies, axes, 0, 0, tiled=True)  47.2 us
    pallas_call x2, Pallas kernels, call_factor(): pl.pallas_call(kernel, out_shape=[jax.ShapeDtypeStruct(shape, jnp.float32...  35.3 us
    all_to_all x4, waiting for transfers between devices, gather(): return lax.all_to_all(copies, axes, 0, 0, tiled=True)  29.4 us
    all_to_all x1, blocking collectives, per_device(): lax.all_to_all(share.reshape(spread, 4, size // 4), ROW, 0, 0, tiled=True)  25.3 us
    all_to_all x1, blocking collectives, per_device(): lax.all_to_all(parts, 'col', 0, 0, tiled=True)  22.3 us
    all_to_all x1, blocking collectives, per_device(): parts = lax.all_to_all(parts, ('y', 'x'), 0, 0, tiled=True)  20.5 us
    all_to_all x4, starting transfers between devices, gather(): return lax.all_to_all(copies, axes, 0, 0, tiled=True)  16.1 us
    all_to_all x1, blocking collectives, per_device(): share = lax.all_to_all(share, ('y', 'col'), 0, 0, tiled=True)  15.4 us
  transfers between devices with their start and end apart: 4, of which 4 were waited for; matrix products, arithmetic and copies ran while one was open for 0% of the time, Pallas kernels for 0%

profile of v3, /device:TPU:1, one launch (start us, length us, event | category | flops | bytes accessed | tf_op | source)
XLA Modules:
  0.0 233.2 jit_solution(13329541516166802635)
XLA Ops:
  0.6 0.0 copy-start
  0.6 1.2 copy-done
  1.9 2.1 abs_reduce_fusion
  4.7 0.1 multiply_convert_fusion
  4.8 0.1 concatenate.6
  4.8 22.3 %all_to_all.65 = f16[8,32,640]{2,1,0:T(8,128)(2,1)S(1)} all-to-all(f16[8,32,640]{2,1,0:T(8,128)(2,1)S(1)} %bitcast.52), channel_id=1, replica_groups=mesh['y'=8,'x'=4,'core'=2,'col'=8] {'col'}, dimensions={0} | all-to-all | bytes 655360 | tf_op jit(solution)/shard_map/all_to_all | solution.py:197
  27.2 0.1 copy.28
  27.3 0.1 multiply_reduce_fusion
  27.5 0.6 abs_reduce_fusion.1
  28.8 0.8 broadcast_in_dim.24
  29.6 3.4 %all-to-all-start.1 = ((f16[8,32,640]{2,1,0:T(8,128)(2,1)}), f16[8,32,640]{2,1,0:T(8,128)(2,1)S(1)}, u32[]{:S(2)}, u32[]{:S(2)}) async-start(f16[8,32,640]{2,1,0:T(8,128)(2,1)} %broadcast_in_dim.24), calls=%async_computation.1 | async-start | bytes 655360 | tf_op jit(solution)/shard_map/all_to_all | solution.py:155
  33.0 9.9 %all-to-all-done.1 = f16[8,32,640]{2,1,0:T(8,128)(2,1)S(1)} async-done(((f16[8,32,640]{2,1,0:T(8,128)(2,1)}), f16[8,32,640]{2,1,0:T(8,128)(2,1)S(1)}, u32[]{:S(2)}, u32[]{:S(2)}) %all-to-all-start.1) | async-done | bytes 327712 | tf_op jit(solution)/shard_map/all_to_all | solution.py:155
  42.9 0.1 copy.29
  43.1 0.1 convert_multiply_fusion
  43.2 0.2 copy.23
  43.4 0.0 copy-start.1
  43.4 1.0 fusion
  44.4 0.1 constant_dynamic-slice_fusion
  44.6 25.3 %all_to_all.66 = f32[64,4,128]{2,1,0:T(4,128)S(1)} all-to-all(f32[64,4,128]{2,1,0:T(4,128)S(1)} %bitcast.56), channel_id=1, replica_groups=mesh['y'=8,'x'=4,'core'=2,'col'=8] {'y','x','core'}, dimensions={0} | all-to-all | bytes 262144 | tf_op jit(solution)/shard_map/all_to_all | solution.py:202
  69.9 0.1 reduce_sum.46
  70.0 15.3 %all_to_all.67 = f32[64,4,128]{2,1,0:T(4,128)S(1)} all-to-all(f32[64,4,128]{2,1,0:T(4,128)S(1)} %broadcast_in_dim.25), channel_id=1, replica_groups=mesh['y'=8,'x'=4,'core'=2,'col'=8] {'y','col'}, dimensions={0} | all-to-all | bytes 262144 | tf_op jit(solution)/shard_map/all_to_all | solution.py:155
  85.3 0.9 broadcast_in_dim.27
  86.1 3.5 %all-to-all-start.4 = ((f32[4,64,512]{2,1,0:T(8,128)}), f32[4,64,512]{2,1,0:T(8,128)S(1)}, u32[]{:S(2)}, u32[]{:S(2)}) async-start(f32[4,64,512]{2,1,0:T(8,128)} %broadcast_in_dim.27), calls=%async_computation.4 | async-start | bytes 1048576 | tf_op jit(solution)/shard_map/all_to_all | solution.py:155
  89.6 0.0 copy-done.1
  89.6 0.2 copy.24
  89.8 6.8 %all-to-all-done.4 = f32[4,64,512]{2,1,0:T(8,128)S(1)} async-done(((f32[4,64,512]{2,1,0:T(8,128)}), f32[4,64,512]{2,1,0:T(8,128)S(1)}, u32[]{:S(2)}, u32[]{:S(2)}) %all-to-all-start.4) | async-done | bytes 524320 | tf_op jit(solution)/shard_map/all_to_all | solution.py:155
  96.6 0.1 broadcast_in_dim.29
  96.7 7.6 %all_to_all.68 = f32[2,256,512]{2,1,0:T(8,128)S(1)} all-to-all(f32[2,256,512]{2,1,0:T(8,128)S(1)} %broadcast_in_dim.29), channel_id=1, replica_groups=mesh['y'=8,'x'=4,'core'=2,'col'=8] {'core'}, dimensions={0} | all-to-all | bytes 2097152 | tf_op jit(solution)/shard_map/all_to_all | solution.py:155
  104.3 17.9 %shard_map.49 = (f32[256,512]{1,0:T(8,128)S(1)}, f32[2,512,512]{2,1,0:T(8,128)S(1)}) custom-call(f32[512,512]{1,0:T(8,128)S(1)} %bitcast.44, f32[256,512]{1,0:T(8,128)S(1)} %bitcast.43, bf16[1024,256]{1,0:T(8,128)(2,1)S(1)} %bitcast.46), custom_call_target="tpu_custom_call" | custom-call | flops 268435456 | bytes 2097152 | tf_op jit(solution)/shard_map/pallas_call | solution.py:140
  122.3 6.3 %all_to_all.69 = f32[2,512,512]{2,1,0:T(8,128)} all-to-all(f32[2,512,512]{2,1,0:T(8,128)S(1)} %get-tuple-element.8), channel_id=1, replica_groups=mesh['y'=8,'x'=4,'core'=2,'col'=8] {'core'}, dimensions={0} | all-to-all | bytes 4194304 | tf_op jit(solution)/shard_map/all_to_all | solution.py:213
  128.6 1.8 reduce_sum.47
  130.4 20.5 %all_to_all.70 = bf16[32,16,512]{2,1,0:T(8,128)(2,1)S(1)} all-to-all(bf16[32,16,512]{2,1,0:T(8,128)(2,1)S(1)} %bitcast.49), channel_id=1, replica_groups=mesh['y'=8,'x'=4,'core'=2,'col'=8] {'y','x'}, dimensions={0} | all-to-all | bytes 1048576 | tf_op jit(solution)/shard_map/all_to_all | solution.py:215
  150.9 0.1 convert_reduce_fusion.tall_ref
  151.0 0.7 broadcast_in_dim.60
  151.7 5.8 %all-to-all-start.8 = ((f32[8,16,512]{2,1,0:T(8,128)}), f32[8,16,512]{2,1,0:T(8,128)S(1)}, u32[]{:S(2)}, u32[]{:S(2)}) async-start(f32[8,16,512]{2,1,0:T(8,128)} %broadcast_in_dim.60), calls=%async_computation.8 | async-start | bytes 524288 | tf_op jit(solution)/shard_map/all_to_all | solution.py:155
  157.5 6.5 %all-to-all-done.8 = f32[8,16,512]{2,1,0:T(8,128)S(1)} async-done(((f32[8,16,512]{2,1,0:T(8,128)}), f32[8,16,512]{2,1,0:T(8,128)S(1)}, u32[]{:S(2)}, u32[]{:S(2)}) %all-to-all-start.8) | async-done | bytes 262176 | tf_op jit(solution)/shard_map/all_to_all | solution.py:155
  164.0 0.1 copy.26
  164.1 0.5 fusion.2
  164.6 0.1 copy.27
  164.7 15.4 %all_to_all.71 = f32[64,4,128]{2,1,0:T(4,128)S(1)} all-to-all(f32[64,4,128]{2,1,0:T(4,128)S(1)} %copy.27), channel_id=1, replica_groups=mesh['y'=8,'x'=4,'core'=2,'col'=8] {'y','col'}, dimensions={0} | all-to-all | bytes 262144 | tf_op jit(solution)/shard_map/all_to_all | solution.py:222
  180.1 0.1 reduce_sum.49
  180.2 15.4 %all_to_all.72 = f32[64,4,128]{2,1,0:T(4,128)S(1)} all-to-all(f32[64,4,128]{2,1,0:T(4,128)S(1)} %broadcast_in_dim.61), channel_id=1, replica_groups=mesh['y'=8,'x'=4,'core'=2,'col'=8] {'y','col'}, dimensions={0} | all-to-all | bytes 262144 | tf_op jit(solution)/shard_map/all_to_all | solution.py:155
  195.6 0.9 broadcast_in_dim.63
  196.5 3.5 %all-to-all-start.11 = ((f32[4,64,512]{2,1,0:T(8,128)}), f32[4,64,512]{2,1,0:T(8,128)S(1)}, u32[]{:S(2)}, u32[]{:S(2)}) async-start(f32[4,64,512]{2,1,0:T(8,128)} %broadcast_in_dim.63), calls=%async_computation.11 | async-start | bytes 1048576 | tf_op jit(solution)/shard_map/all_to_all | solution.py:155
  200.0 0.6 dynamic-slice_multiply_fusion
  200.6 6.3 %all-to-all-done.11 = f32[4,64,512]{2,1,0:T(8,128)S(1)} async-done(((f32[4,64,512]{2,1,0:T(8,128)}), f32[4,64,512]{2,1,0:T(8,128)S(1)}, u32[]{:S(2)}, u32[]{:S(2)}) %all-to-all-start.11) | async-done | bytes 524320 | tf_op jit(solution)/shard_map/all_to_all | solution.py:155
  206.9 0.1 broadcast_in_dim.65
  207.0 8.9 %all_to_all.73 = f32[2,256,512]{2,1,0:T(8,128)S(1)} all-to-all(f32[2,256,512]{2,1,0:T(8,128)S(1)} %broadcast_in_dim.65), channel_id=1, replica_groups=mesh['y'=8,'x'=4,'core'=2,'col'=8] {'core'}, dimensions={0} | all-to-all | bytes 2097152 | tf_op jit(solution)/shard_map/all_to_all | solution.py:155
  215.9 17.4 %shard_map.50 = (f32[16,512]{1,0:T(8,128)}, f32[512,512]{1,0:T(8,128)}) custom-call(f32[512,512]{1,0:T(8,128)S(1)} %bitcast.45, f32[16,512]{1,0:T(8,128)S(1)} %convert_reduce_fusion.tall_ref), custom_call_target="tpu_custom_call" | custom-call | flops 268435456 | bytes 2097152 | tf_op jit(solution)/shard_map/pallas_call | solution.py:140
  (10 shorter events, 0.1 us)
Async XLA Ops:
  0.6 1.2 copy-start
  29.6 13.3 %all-to-all-start.1 = ((f16[8,32,640]{2,1,0:T(8,128)(2,1)}), f16[8,32,640]{2,1,0:T(8,128)(2,1)S(1)}, u32[]{:S(2)}, u32[]{:S(2)}) async-start(f16[8,32,640]{2,1,0:T(8,128)(2,1)} %broadcast_in_dim.24), calls=%async_computation.1 | async-start | bytes 655360 | tf_op jit(solution)/shard_map/all_to_all | solution.py:155
  43.4 46.2 %copy-start.1 = (bf16[256,1024]{1,0:T(8,128)(2,1)S(1)}, bf16[256,1024]{1,0:T(8,128)(2,1)}, u32[]{:S(2)}) copy-start(bf16[256,1024]{1,0:T(8,128)(2,1)} %param.2) | copy-start | bytes 1572868
  86.1 10.5 %all-to-all-start.4 = ((f32[4,64,512]{2,1,0:T(8,128)}), f32[4,64,512]{2,1,0:T(8,128)S(1)}, u32[]{:S(2)}, u32[]{:S(2)}) async-start(f32[4,64,512]{2,1,0:T(8,128)} %broadcast_in_dim.27), calls=%async_computation.4 | async-start | bytes 1048576 | tf_op jit(solution)/shard_map/all_to_all | solution.py:155
  151.7 12.3 %all-to-all-start.8 = ((f32[8,16,512]{2,1,0:T(8,128)}), f32[8,16,512]{2,1,0:T(8,128)S(1)}, u32[]{:S(2)}, u32[]{:S(2)}) async-start(f32[8,16,512]{2,1,0:T(8,128)} %broadcast_in_dim.60), calls=%async_computation.8 | async-start | bytes 524288 | tf_op jit(solution)/shard_map/all_to_all | solution.py:155
  196.5 10.4 %all-to-all-start.11 = ((f32[4,64,512]{2,1,0:T(8,128)}), f32[4,64,512]{2,1,0:T(8,128)S(1)}, u32[]{:S(2)}, u32[]{:S(2)}) async-start(f32[4,64,512]{2,1,0:T(8,128)} %broadcast_in_dim.63), calls=%async_computation.11 | async-start | bytes 1048576 | tf_op jit(solution)/shard_map/all_to_all | solution.py:155
